TPU v7x, 256 devices: a whole 4x4x8 slice. The times are simulated.
256 devices in a mesh: space: 64 (over x, y_hi, z), mode: 4 (over y_lo, core).
Axes of the slice: x: 4, y: 4 (y_hi: 2, y_lo: 2; y = y_hi * 2 + y_lo), z: 8, core: 2. Of those that a mesh axis runs over, the one named last changes fastest.
Arguments:
- chaos_field: float32 [84, 64, 128, 128], P('mode', 'space'), may hold values from -6 to 6
- mean_field: float32 [64, 128, 128], P('space'), may hold values from 0.5 to 2
- kl_fields: float32 [6, 64, 128, 128], P(None, 'space'), may hold values from -1.8 to 1.8
- pattern: int32 [7, 84, 84], replicated, may hold values from 0 to 1, as said below
- coupling: float32 [7, 84, 84], replicated, as said below
- slot_mode: int32 [84], replicated, may hold values from 0 to 83, each once
Outputs:
- product: float32 [84, 64, 128, 128], P('mode', 'space')
Inputs may be any that keep to these rules, and one draw needn't show every extreme that they name: Modes are the 84 multi-indices of total degree at most 3 in 6 variables; pattern[0] is the identity; each term k >= 1 belongs to one variable, each variable to one term, and pattern[k, a, b] is 1 exactly where the multi-indices of modes a and b differ by one in that variable and agree elsewhere. coupling[0] is the identity; for k >= 1, coupling[k, a, b] is the square root of the larger of the two degrees in the term's variable where pattern[k, a, b] is 1, and zero elsewhere; pattern and coupling name the same variable for each term. `slot_mode`: each slot holds a different chaos mode.
All inputs are finite; a program needn't handle non-finite values.
Results may differ from a plain program's by a relative error of at most 0.000082.
Values sent between devices are 32-bit elements; how exact they have to be, the bound alone decides.
A program may use at most 320 MiB of HBM per device.

v0:
```python
import jax
import jax.numpy as jnp
from jax import lax
from jax.experimental import pallas as pl
from jax.experimental.pallas import tpu as pltpu
from jax.sharding import PartitionSpec as P

MESH = pl.DeviceIdType.MESH
RING = 8
GROUPS = 4
QUOTA = 21
SLOTS = GROUPS * QUOTA
TERMS = 7
ROWS = 8
PAD = 24
DEPTH = 176
SIDE = 128
CHUNKS = SIDE // ROWS
PAIRS = CHUNKS // 2
F32 = jnp.float32
BF16 = jnp.bfloat16


def split(value):
    high = value.astype(BF16)
    return high, (value - high.astype(F32)).astype(BF16)


def dot(left, right):
    return jnp.dot(left, right, preferred_element_type=F32)


def iota(shape, dim):
    return lax.broadcasted_iota(jnp.int32, shape, dim)


def over_pad(index):
    return (index * 43691) >> 20


def build_mixing(groups, pattern, coupling, slots, mixing):
    of_mode = (iota((SLOTS, SLOTS), 0) == slots[...]).astype(BF16)
    row, col = iota((GROUPS * PAD, SLOTS), 0), iota((GROUPS * PAD, SLOTS), 1)
    part = over_pad(row)
    inner = row - part * PAD
    pick = ((col == part * QUOTA + inner) & (inner < QUOTA)).astype(BF16)
    left = lax.dot_general(
        pick, of_mode, (((1,), (1,)), ((), ())), preferred_element_type=F32
    ).astype(BF16)
    row, col = iota((SLOTS, DEPTH), 0), iota((SLOTS, DEPTH), 1)
    part = over_pad(col)
    inner = col - part * PAD
    rights = []
    for group in groups:
        pick = ((row == group * QUOTA + inner) & (inner < QUOTA)).astype(BF16)
        rights.append(dot(of_mode, pick).astype(BF16))
    term = over_pad(iota((GROUPS * PAD, DEPTH), 1))
    totals = [[jnp.zeros((GROUPS * PAD, DEPTH), F32)] * 2 for _ in groups]
    for k in range(TERMS):
        masked = coupling[k] * pattern[k].astype(F32)
        for level, part in enumerate(split(masked)):
            rows = dot(left, part).astype(BF16)
            for i, right in enumerate(rights):
                totals[i][level] = jnp.where(term == k, dot(rows, right), totals[i][level])
    for i in range(len(groups)):
        for level in range(2):
            mixing[i, level] = totals[i][level].astype(BF16)


def mix(mixing, i, values):
    high, low = split(values)
    return (
        dot(mixing[i, 0], high) + dot(mixing[i, 1], high) + dot(mixing[i, 0], low)
    )


def slots_inside(block):
    zeros = jnp.zeros((PAD - QUOTA, ROWS, SIDE), F32)
    return jnp.swapaxes(jnp.concatenate([block, zeros], 0), 0, 1)


def kernel(
    u_hbm, mean_hbm, kl_hbm, pattern_hbm, coupling_hbm, slots_hbm, own_out, far_out,
    field, turned, coef, pattern, coupling, slots, mixing, halo, edge, weight, centre, partial, near,
    load_sem, store_sem,
    halo_send, halo_recv, edge_send, edge_recv, pass_send, pass_recv, near_send, near_recv, far_send, far_recv,
):
    place = lax.axis_index("space")
    mode = lax.axis_index("mode")
    planes = lax.axis_size("space")
    core = mode % 2
    sibling = mode + 1 - 2 * core
    across = (mode + 2) % 4
    diagonal = (sibling + 2) % 4
    along = place % RING
    mode_up = jnp.where(along == RING - 1, across, mode)
    mode_down = jnp.where(along == 0, across, mode)
    has_up = place < planes - 1
    has_down = place > 0
    up = (place + 1, mode_up)
    down = (place - 1, mode_down)
    sends = ((has_up, up), (has_down, down))
    comes = (has_down, has_up)

    loads = [
        pltpu.make_async_copy(u_hbm.at[:, 0], field, load_sem.at[0]),
        pltpu.make_async_copy(mean_hbm, coef.at[pl.ds(0, 1), pl.ds(ROWS, SIDE)], load_sem.at[1]),
        pltpu.make_async_copy(kl_hbm.at[:, 0], coef.at[pl.ds(1, TERMS - 1), pl.ds(ROWS, SIDE)], load_sem.at[2]),
        pltpu.make_async_copy(pattern_hbm, pattern, load_sem.at[3]),
        pltpu.make_async_copy(coupling_hbm, coupling, load_sem.at[4]),
        pltpu.make_async_copy(slots_hbm, slots, load_sem.at[5]),
    ]
    for i in (1, 2, 0, 3, 4, 5):
        loads[i].start()

    barrier = pltpu.get_barrier_semaphore()

    def greet(device):
        pl.semaphore_signal(barrier, inc=1, device_id=device, device_id_type=MESH)

    for there, device in sends:
        pl.when(there)(lambda device=device: greet(device))
    greet((place, sibling))
    greet((place, across))

    zero_rows = jnp.zeros((TERMS, ROWS, SIDE), F32)
    coef[:, pl.ds(0, ROWS)] = zero_rows
    coef[:, pl.ds(ROWS + SIDE, ROWS)] = zero_rows
    turned[0] = jnp.zeros((PAD, SIDE), F32)
    turned[SIDE + 1] = jnp.zeros((PAD, SIDE), F32)

    for h in range(2):

        @pl.when(jnp.logical_not(comes[h]))
        def _():
            @pl.loop(0, CHUNKS)
            def _(j):
                halo[h, j] = jnp.zeros((QUOTA, ROWS, SIDE), F32)
                edge[h, j] = zero_rows

    loads[1].wait()
    loads[2].wait()
    pl.semaphore_wait(barrier, 2 + has_up.astype(jnp.int32) + has_down.astype(jnp.int32))

    def halo_copy(h, j):
        return pltpu.make_async_remote_copy(
            src_ref=u_hbm.at[:, 0, pl.ds(pl.multiple_of(j * ROWS, ROWS), ROWS)],
            dst_ref=halo.at[h, j],
            send_sem=halo_send.at[h, j],
            recv_sem=halo_recv.at[h, j],
            device_id=sends[h][1],
            device_id_type=MESH,
        )

    def edge_copy(h, p):
        j = 2 * p + core
        return pltpu.make_async_remote_copy(
            src_ref=coef.at[:, pl.ds(pl.multiple_of(ROWS + j * ROWS, ROWS), ROWS)],
            dst_ref=edge.at[h, j],
            send_sem=edge_send.at[h, p],
            recv_sem=edge_recv.at[h, p],
            device_id=sends[h][1],
            device_id_type=MESH,
        )

    def pass_copy(h, p, mine):
        j = 2 * p + (core if mine else 1 - core)
        return pltpu.make_async_remote_copy(
            src_ref=edge.at[h, j],
            dst_ref=edge.at[h, j],
            send_sem=pass_send.at[h, p],
            recv_sem=pass_recv.at[h, p],
            device_id=(place, sibling),
            device_id_type=MESH,
        )

    def near_copy(i, j):
        return pltpu.make_async_remote_copy(
            src_ref=partial.at[j, (sibling, diagonal)[i]],
            dst_ref=near.at[j, i],
            send_sem=near_send.at[i, j],
            recv_sem=near_recv.at[i, j],
            device_id=(place, sibling),
            device_id_type=MESH,
        )

    def rows_of(j):
        return pl.ds(pl.multiple_of(j * ROWS, ROWS), ROWS)

    def far_copy(j):
        return pltpu.make_async_remote_copy(
            src_ref=partial.at[j, across],
            dst_ref=far_out.at[:, rows_of(j)],
            send_sem=far_send.at[j],
            recv_sem=far_recv.at[j],
            device_id=(place, across),
            device_id_type=MESH,
        )

    def own_copy(j):
        return pltpu.make_async_copy(partial.at[j, mode], own_out.at[:, rows_of(j)], store_sem.at[j])

    for h in range(2):
        pl.when(sends[h][0])(lambda h=h: edge_copy(h, 0).start())

    @pl.loop(0, PAIRS)
    def _(p):
        for h in range(2):

            @pl.when(sends[h][0])
            def _():
                @pl.when(p < PAIRS - 1)
                def _():
                    edge_copy(h, p + 1).start()

                halo_copy(h, 2 * p).start()

        for h in range(2):
            pl.when(sends[h][0])(lambda h=h: halo_copy(h, 2 * p + 1).start())

    loads[3].wait()
    loads[4].wait()
    loads[5].wait()
    build_mixing((mode, mode_down, mode_up), pattern, coupling, slots, mixing)
    loads[0].wait()

    @pl.loop(0, CHUNKS)
    def _(j):
        turned[pl.ds(j * ROWS + 1, ROWS)] = slots_inside(field[:, rows_of(j)])

    def relay_edges(p):
        for h in range(2):

            @pl.when(comes[h])
            def _():
                edge_copy(h, p).wait_recv()
                pass_copy(h, p, True).start()

    def take_edges(p):
        for h in range(2):
            pl.when(comes[h])(lambda h=h: pass_copy(h, p, False).wait_recv())

    first = iota((1, 1, SIDE), 2) == 0
    last = iota((1, 1, SIDE), 2) == SIDE - 1

    def own_part(j):
        block = coef[:, pl.ds(pl.multiple_of(j * ROWS, ROWS), 3 * ROWS)]
        here = block[:, ROWS : 2 * ROWS]
        right = 0.5 * (here + jnp.where(last, 0.0, pltpu.roll(here, SIDE - 1, 2)))
        left = 0.5 * (here + jnp.where(first, 0.0, pltpu.roll(here, 1, 2)))
        after = 0.5 * (here + block[:, ROWS + 1 : 2 * ROWS + 1])
        before = 0.5 * (here + block[:, ROWS - 1 : 2 * ROWS - 1])
        below = 0.5 * (here + edge[0, j])
        above = 0.5 * (here + edge[1, j])
        weight[0] = right + left + after + before + below + above
        weight[1] = jnp.where(last, 0.0, -right)
        weight[2] = jnp.where(first, 0.0, -left)
        weight[3] = -after
        weight[4] = -before
        weight[5] = -below
        weight[6] = -above
        for r in range(0, ROWS, 2):
            sides = []
            for q in (r, r + 1):
                y = j * ROWS + q + 1
                own = turned[y]
                values = (own, pltpu.roll(own, SIDE - 1, 1), pltpu.roll(own, 1, 1), turned[y + 1], turned[y - 1])
                terms = []
                for k in range(TERMS):
                    total = weight[0, k, q : q + 1] * values[0]
                    for i in range(1, 5):
                        total = total + weight[i, k, q : q + 1] * values[i]
                    terms.append(total)
                sides.append(jnp.concatenate(terms + [jnp.zeros((DEPTH - TERMS * PAD, SIDE), F32)], 0))
            mixed = mix(mixing, 0, jnp.concatenate(sides, 1))
            centre[r] = mixed[:, :SIDE]
            centre[r + 1] = mixed[:, SIDE:]

    def halo_part(j):
        for h in range(2):
            pl.when(comes[h])(lambda h=h: halo_copy(h, j).wait_recv())
        beside = [slots_inside(halo[h, j]) for h in range(2)]
        results = []
        for r in range(0, ROWS, 2):
            mixed = jnp.concatenate([centre[r], centre[r + 1]], 1)
            for h in range(2):
                sides = []
                for q in (r, r + 1):
                    terms = [weight[5 + h, k, q : q + 1] * beside[h][q] for k in range(TERMS)]
                    sides.append(jnp.concatenate(terms + [jnp.zeros((DEPTH - TERMS * PAD, SIDE), F32)], 0))
                mixed = mixed + mix(mixing, 1 + h, jnp.concatenate(sides, 1))
            results.extend([mixed[None, :, :SIDE], mixed[None, :, SIDE:]])
        by_slot = jnp.swapaxes(jnp.concatenate(results, 0), 0, 1)
        for g in range(GROUPS):
            partial[j, g] = by_slot[g * PAD : g * PAD + QUOTA]
        near_copy(1, j).start()
        near_copy(0, j).start()

    def join(j):
        near_copy(1, j).wait_recv()
        partial[j, across] = partial[j, across] + near[j, 1]
        far_copy(j).start()
        near_copy(0, j).wait_recv()
        partial[j, mode] = partial[j, mode] + near[j, 0]
        own_copy(j).start()

    relay_edges(0)
    take_edges(0)
    own_part(0)

    @pl.loop(0, PAIRS)
    def _(p):
        halo_part(2 * p)
        pl.when(p < PAIRS - 1)(lambda: relay_edges(p + 1))
        own_part(2 * p + 1)
        join(2 * p)
        halo_part(2 * p + 1)

        @pl.when(p < PAIRS - 1)
        def _():
            take_edges(p + 1)
            own_part(2 * p + 2)

        join(2 * p + 1)

    @pl.loop(0, PAIRS)
    def _(p):
        for h in range(2):

            @pl.when(sends[h][0])
            def _():
                edge_copy(h, p).wait_send()
                halo_copy(h, 2 * p).wait_send()
                halo_copy(h, 2 * p + 1).wait_send()

            pl.when(comes[h])(lambda h=h: pass_copy(h, p, True).wait_send())

    @pl.loop(0, CHUNKS)
    def _(j):
        for i in range(2):
            near_copy(i, j).wait_send()
        far_copy(j).wait()
        own_copy(j).wait()


def on_device(chaos_field, mean_field, kl_fields, pattern, coupling, slot_mode):
    dma = pltpu.SemaphoreType.DMA
    result = pltpu.VMEM((QUOTA, SIDE, SIDE), F32)
    operands = (chaos_field, mean_field, kl_fields, pattern, coupling, slot_mode.reshape(1, SLOTS))
    operands = [pltpu.with_memory_space_constraint(operand, pltpu.HBM) for operand in operands]
    own, far = pl.pallas_call(
        kernel,
        out_shape=(result, result),
        in_specs=[pl.BlockSpec(memory_space=pltpu.HBM)] * len(operands),
        out_specs=(pl.BlockSpec(memory_space=pl.ANY),) * 2,
        scratch_shapes=[
            pltpu.VMEM((QUOTA, SIDE, SIDE), F32),
            pltpu.VMEM((SIDE + 2, PAD, SIDE), F32),
            pltpu.VMEM((TERMS, SIDE + 2 * ROWS, SIDE), F32),
            pltpu.VMEM((TERMS, SLOTS, SLOTS), jnp.int32),
            pltpu.VMEM((TERMS, SLOTS, SLOTS), F32),
            pltpu.VMEM((1, SLOTS), jnp.int32),
            pltpu.VMEM((3, 2, GROUPS * PAD, DEPTH), BF16),
            pltpu.VMEM((2, CHUNKS, QUOTA, ROWS, SIDE), F32),
            pltpu.VMEM((2, CHUNKS, TERMS, ROWS, SIDE), F32),
            pltpu.VMEM((7, TERMS, ROWS, SIDE), F32),
            pltpu.VMEM((ROWS, GROUPS * PAD, SIDE), F32),
            pltpu.VMEM((CHUNKS, GROUPS, QUOTA, ROWS, SIDE), F32),
            pltpu.VMEM((CHUNKS, 2, QUOTA, ROWS, SIDE), F32),
            dma((6,)),
            dma((CHUNKS,)),
            dma((2, CHUNKS)),
            dma((2, CHUNKS)),
            dma((2, PAIRS)),
            dma((2, PAIRS)),
            dma((2, PAIRS)),
            dma((2, PAIRS)),
            dma((2, CHUNKS)),
            dma((2, CHUNKS)),
            dma((CHUNKS,)),
            dma((CHUNKS,)),
        ],
        compiler_params=pltpu.CompilerParams(
            collective_id=0, has_side_effects=True, vmem_limit_bytes=40 << 20
        ),
    )(*operands)
    return (own + far).reshape(QUOTA, 1, SIDE, SIDE)


def solution(mesh):
    in_specs = (
        P("mode", "space", None, None),
        P("space", None, None),
        P(None, "space", None, None),
        P(),
        P(),
        P(),
    )
    out_specs = P("mode", "space", None, None)
    return jax.shard_map(
        on_device, mesh=mesh, in_specs=in_specs, out_specs=out_specs, check_vma=False
    )
```

profile of v0, /device:TPU:6, one launch (start us, length us, event | category | flops | bytes accessed | tf_op | source)
XLA Modules:
  0.0 53.9 jit_solution(3780165345865203784)
XLA Ops:
  0.0 52.7 %shard_map.64 = (f32[21,128,128]{2,1,0:T(8,128)S(1)}, f32[21,128,128]{2,1,0:T(8,128)S(1)}) custom-call(f32[21,1,128,128]{3,2,1,0:T(8,128)} %u_hbm.1, f32[1,128,128]{2,1,0:T(8,128)} %mean_hbm.1, f32[6,1,128,128]{3,2,1,0:T(8,128)} %kl_hbm.1, s32[7,84,84]{2,1,0:T(8,128)} %pattern_hbm.1, f32[7,84,84]{2,1,0:T(8,128)} %coupling_hbm.1, s32[1,84]{1,0:T(1,128)} %bitcast.5), custom_call_target="tpu_custom_call" | custom-call | tf_op jit(solution)/shard_map/pallas_call | solution.py:351
  52.7 1.3 %add_bitcast_fusion = f32[21,1,128,128]{3,2,1,0:T(8,128)} fusion(f32[21,128,128]{2,1,0:T(8,128)S(1)} %get-tuple-element.7, f32[21,128,128]{2,1,0:T(8,128)S(1)} %get-tuple-element.8), kind=kLoop, calls=%fused_computation | loop fusion | flops 344064 | bytes 4128768 | tf_op jit(solution)/shard_map/reshape | solution.py:387
where the time goes:
time: 54.1 us; the launch traced here: 53.9 us
  Pallas kernels  52.7 us (97%)
  other arithmetic  1.27 us (2%)
    pallas_call x1, Pallas kernels, on_device(): pl.pallas_call(kernel, out_shape=(result, result), in_specs=[pl.BlockSpec...  52.7 us
    reshape x1, other arithmetic, on_device(): return (own + far).reshape(QUOTA, 1, SIDE, SIDE)  1.27 us

commit v1 on v0

--- a/solution.py
+++ b/solution.py
@@ -17,6 +17,12 @@
 SIDE = 128
 CHUNKS = SIDE // ROWS
 PAIRS = CHUNKS // 2
+LATE = 4
+EARLY = CHUNKS - LATE
+LOOPS = EARLY // 2
+GATHERED = LATE + 1
+DENSE = 256
+MIXED = GROUPS * PAD
 F32 = jnp.float32
 BF16 = jnp.bfloat16
 
@@ -38,15 +44,21 @@
     return (index * 43691) >> 20
 
 
-def build_mixing(groups, pattern, coupling, slots, mixing):
+def build_mixing(groups, pattern, coupling, slots, mixing, turned_mixing):
     of_mode = (iota((SLOTS, SLOTS), 0) == slots[...]).astype(BF16)
-    row, col = iota((GROUPS * PAD, SLOTS), 0), iota((GROUPS * PAD, SLOTS), 1)
+    row, col = iota((MIXED, SLOTS), 0), iota((MIXED, SLOTS), 1)
     part = over_pad(row)
     inner = row - part * PAD
     pick = ((col == part * QUOTA + inner) & (inner < QUOTA)).astype(BF16)
     left = lax.dot_general(
         pick, of_mode, (((1,), (1,)), ((), ())), preferred_element_type=F32
     ).astype(BF16)
+    row, col = iota((MIXED, DENSE), 0), iota((MIXED, DENSE), 1)
+    part = over_pad(row)
+    inner = row - part * PAD
+    again = (col >= SLOTS).astype(jnp.int32) + (col >= 2 * SLOTS).astype(jnp.int32)
+    dense = (col - again * SLOTS == part * QUOTA + inner) & (inner < QUOTA)
+    dense = [(dense & (again < 2)).astype(BF16), (dense & (again == 2)).astype(BF16)]
     row, col = iota((SLOTS, DEPTH), 0), iota((SLOTS, DEPTH), 1)
     part = over_pad(col)
     inner = col - part * PAD
@@ -54,8 +66,8 @@
     for group in groups:
         pick = ((row == group * QUOTA + inner) & (inner < QUOTA)).astype(BF16)
         rights.append(dot(of_mode, pick).astype(BF16))
-    term = over_pad(iota((GROUPS * PAD, DEPTH), 1))
-    totals = [[jnp.zeros((GROUPS * PAD, DEPTH), F32)] * 2 for _ in groups]
+    term = over_pad(iota((MIXED, DEPTH), 1))
+    totals = [[jnp.zeros((MIXED, DEPTH), F32)] * 2 for _ in groups]
     for k in range(TERMS):
         masked = coupling[k] * pattern[k].astype(F32)
         for level, part in enumerate(split(masked)):
@@ -63,15 +75,20 @@
             for i, right in enumerate(rights):
                 totals[i][level] = jnp.where(term == k, dot(rows, right), totals[i][level])
     for i in range(len(groups)):
+        turned = jnp.zeros((DEPTH, DENSE), F32)
         for level in range(2):
-            mixing[i, level] = totals[i][level].astype(BF16)
+            matrix = totals[i][level].astype(BF16)
+            mixing[i, level * MIXED : (level + 1) * MIXED] = matrix
+            turned = turned + lax.dot_general(
+                matrix, dense[level], (((0,), (0,)), ((), ())), preferred_element_type=F32
+            )
+        turned_mixing[i] = turned.astype(BF16)
 
 
 def mix(mixing, i, values):
     high, low = split(values)
-    return (
-        dot(mixing[i, 0], high) + dot(mixing[i, 1], high) + dot(mixing[i, 0], low)
-    )
+    both = dot(mixing[i], high)
+    return both[:MIXED] + both[MIXED:] + dot(mixing[i, :MIXED], low)
 
 
 def slots_inside(block):
@@ -81,8 +98,10 @@
 
 def kernel(
     u_hbm, mean_hbm, kl_hbm, pattern_hbm, coupling_hbm, slots_hbm, own_out, far_out,
-    field, turned, coef, pattern, coupling, slots, mixing, halo, edge, weight, centre, partial, near,
-    load_sem, store_sem,
+    field, turned, coef, pattern, coupling, slots, mixing, turned_mixing, halo, edge, weight, centre, partial, near,
+    gathered, dense, mixed_rows, blank,
+    load_sem, store_sem, blank_sem,
+    gather_send, gather_recv,
     halo_send, halo_recv, edge_send, edge_recv, pass_send, pass_recv, near_send, near_recv, far_send, far_recv,
 ):
     place = lax.axis_index("space")
@@ -200,28 +219,56 @@
     def own_copy(j):
         return pltpu.make_async_copy(partial.at[j, mode], own_out.at[:, rows_of(j)], store_sem.at[j])
 
-    for h in range(2):
-        pl.when(sends[h][0])(lambda h=h: edge_copy(h, 0).start())
-
-    @pl.loop(0, PAIRS)
+    def send_edges(p):
+        for h in range(2):
+            pl.when(sends[h][0])(lambda h=h: edge_copy(h, p).start())
+
+    def gather_copy(i, c):
+        rows = pl.ds(pl.multiple_of((EARLY - 1 + c) * ROWS, ROWS), ROWS)
+        group = (mode, mode, across)[i]
+        return pltpu.make_async_remote_copy(
+            src_ref=gathered.at[c, group] if i == 2 else u_hbm.at[:, 0, rows],
+            dst_ref=gathered.at[c, group],
+            send_sem=gather_send.at[i, c],
+            recv_sem=gather_recv.at[i, c],
+            device_id=(place, (across, sibling, sibling)[i]),
+            device_id_type=MESH,
+        )
+
+    def late_copy(h, c):
+        return pltpu.make_async_remote_copy(
+            src_ref=partial.at[EARLY + c, h],
+            dst_ref=halo.at[h, EARLY + c],
+            send_sem=halo_send.at[h, EARLY + c],
+            recv_sem=halo_recv.at[h, EARLY + c],
+            device_id=sends[h][1],
+            device_id_type=MESH,
+        )
+
+    send_edges(0)
+
+    @pl.loop(0, LOOPS)
     def _(p):
-        for h in range(2):
-
-            @pl.when(sends[h][0])
-            def _():
-                @pl.when(p < PAIRS - 1)
-                def _():
-                    edge_copy(h, p + 1).start()
-
-                halo_copy(h, 2 * p).start()
-
-        for h in range(2):
-            pl.when(sends[h][0])(lambda h=h: halo_copy(h, 2 * p + 1).start())
+        pl.when(p < LOOPS - 1)(lambda: send_edges(p + 1))
+        pl.when((p == 1) | (p == 2))(lambda: send_edges(LOOPS + p - 1))
+        for j in (2 * p, 2 * p + 1):
+            for h in range(2):
+                pl.when(sends[h][0])(lambda h=h, j=j: halo_copy(h, j).start())
+
+    @pl.loop(0, GATHERED)
+    def _(c):
+        gather_copy(0, c).start()
+        gather_copy(1, c).start()
+
+    blank[...] = jnp.zeros_like(blank)
+    blank_copy = pltpu.make_async_copy(blank, far_out.at[:, pl.ds(EARLY * ROWS, LATE * ROWS)], blank_sem)
+    blank_copy.start()
+    dense[GATHERED * ROWS] = jnp.zeros((DENSE, SIDE), BF16)
 
     loads[3].wait()
     loads[4].wait()
     loads[5].wait()
-    build_mixing((mode, mode_down, mode_up), pattern, coupling, slots, mixing)
+    build_mixing((mode, mode_down, mode_up), pattern, coupling, slots, mixing, turned_mixing)
     loads[0].wait()
 
     @pl.loop(0, CHUNKS)
@@ -243,7 +290,7 @@
     first = iota((1, 1, SIDE), 2) == 0
     last = iota((1, 1, SIDE), 2) == SIDE - 1
 
-    def own_part(j):
+    def set_weights(slot, j):
         block = coef[:, pl.ds(pl.multiple_of(j * ROWS, ROWS), 3 * ROWS)]
         here = block[:, ROWS : 2 * ROWS]
         right = 0.5 * (here + jnp.where(last, 0.0, pltpu.roll(here, SIDE - 1, 2)))
@@ -252,13 +299,16 @@
         before = 0.5 * (here + block[:, ROWS - 1 : 2 * ROWS - 1])
         below = 0.5 * (here + edge[0, j])
         above = 0.5 * (here + edge[1, j])
-        weight[0] = right + left + after + before + below + above
-        weight[1] = jnp.where(last, 0.0, -right)
-        weight[2] = jnp.where(first, 0.0, -left)
-        weight[3] = -after
-        weight[4] = -before
-        weight[5] = -below
-        weight[6] = -above
+        weight[slot, 0] = right + left + after + before + below + above
+        weight[slot, 1] = jnp.where(last, 0.0, -right)
+        weight[slot, 2] = jnp.where(first, 0.0, -left)
+        weight[slot, 3] = -after
+        weight[slot, 4] = -before
+        weight[slot, 5] = -below
+        weight[slot, 6] = -above
+
+    def own_part(j):
+        set_weights(0, j)
         for r in range(0, ROWS, 2):
             sides = []
             for q in (r, r + 1):
@@ -267,9 +317,9 @@
                 values = (own, pltpu.roll(own, SIDE - 1, 1), pltpu.roll(own, 1, 1), turned[y + 1], turned[y - 1])
                 terms = []
                 for k in range(TERMS):
-                    total = weight[0, k, q : q + 1] * values[0]
+                    total = weight[0, 0, k, q : q + 1] * values[0]
                     for i in range(1, 5):
-                        total = total + weight[i, k, q : q + 1] * values[i]
+                        total = total + weight[0, i, k, q : q + 1] * values[i]
                     terms.append(total)
                 sides.append(jnp.concatenate(terms + [jnp.zeros((DEPTH - TERMS * PAD, SIDE), F32)], 0))
             mixed = mix(mixing, 0, jnp.concatenate(sides, 1))
@@ -286,7 +336,7 @@
             for h in range(2):
                 sides = []
                 for q in (r, r + 1):
-                    terms = [weight[5 + h, k, q : q + 1] * beside[h][q] for k in range(TERMS)]
+                    terms = [weight[0, 5 + h, k, q : q + 1] * beside[h][q] for k in range(TERMS)]
                     sides.append(jnp.concatenate(terms + [jnp.zeros((DEPTH - TERMS * PAD, SIDE), F32)], 0))
                 mixed = mixed + mix(mixing, 1 + h, jnp.concatenate(sides, 1))
             results.extend([mixed[None, :, :SIDE], mixed[None, :, SIDE:]])
@@ -304,43 +354,143 @@
         partial[j, mode] = partial[j, mode] + near[j, 0]
         own_copy(j).start()
 
+    at_end = (along == 0) | (along == RING - 1)
+    other = jnp.where(along == 0, 1, 2)
+    used = (jnp.where(along == RING - 1, 1, 0), jnp.where(along == 0, 1, 0))
+
+    def pass_gathered(c):
+        gather_copy(0, c).wait_recv()
+        gather_copy(2, c).start()
+
+    def turn_gathered(c):
+        gather_copy(1, c).wait_recv()
+        gather_copy(2, c).wait_recv()
+        rows = pl.ds(pl.multiple_of((EARLY - 1 + c) * ROWS, ROWS), ROWS)
+        gathered[c, mode] = field[:, rows]
+        block = gathered[c].reshape(SLOTS, ROWS, SIDE)
+        high = block.astype(BF16).astype(F32)
+        zeros = jnp.zeros((DENSE - 3 * SLOTS, ROWS, SIDE), F32)
+        block = jnp.concatenate([high, block - high, high, zeros], 0)
+        dense[pl.ds(c * ROWS, ROWS)] = jnp.swapaxes(block, 0, 1).astype(BF16)
+
+    def mix_rows(slot, i, c):
+        for r in range(0, ROWS + 2, 2):
+            y = c * ROWS + ROWS - 1 + r
+            mixed = dot(turned_mixing[i], jnp.concatenate([dense[y], dense[y + 1]], 1))
+            mixed_rows[slot, r] = mixed[:, :SIDE]
+            mixed_rows[slot, r + 1] = mixed[:, SIDE:]
+
+    def by_slot(rows):
+        return jnp.swapaxes(jnp.concatenate([row[None] for row in rows], 0), 0, 1)[:QUOTA]
+
+    def late_part(c):
+        set_weights(1, EARLY + c)
+        mix_rows(0, 0, c)
+        pl.when(at_end)(lambda: mix_rows(1, other, c))
+
+        def term(slot, r, k):
+            return mixed_rows[slot, r + 1, k * PAD : (k + 1) * PAD]
+
+        for h in range(2):
+            rows = []
+            for r in range(ROWS):
+                total = weight[1, 6 - h, 0, r : r + 1] * term(used[h], r, 0)
+                for k in range(1, TERMS):
+                    total = total + weight[1, 6 - h, k, r : r + 1] * term(used[h], r, k)
+                rows.append(total)
+            partial[EARLY + c, h] = by_slot(rows)
+            pl.when(sends[h][0])(lambda h=h: late_copy(h, c).start())
+        rows = []
+        for r in range(ROWS):
+            total = jnp.zeros((PAD, SIDE), F32)
+            for k in range(TERMS):
+                own = term(0, r, k)
+                values = (own, pltpu.roll(own, SIDE - 1, 1), pltpu.roll(own, 1, 1), term(0, r + 1, k), term(0, r - 1, k))
+                for i in range(5):
+                    total = total + weight[1, i, k, r : r + 1] * values[i]
+            rows.append(total)
+        partial[EARLY + c, 2] = by_slot(rows)
+
+    def late_join(c):
+        j = EARLY + c
+        for h in range(2):
+            pl.when(comes[h])(lambda h=h: late_copy(h, c).wait_recv())
+        partial[j, 2] = partial[j, 2] + halo[0, j] + halo[1, j]
+        late_store(c).start()
+
+    def late_store(c):
+        j = EARLY + c
+        return pltpu.make_async_copy(partial.at[j, 2], own_out.at[:, rows_of(j)], store_sem.at[j])
+
     relay_edges(0)
     take_edges(0)
     own_part(0)
 
-    @pl.loop(0, PAIRS)
+    @pl.loop(0, LOOPS)
     def _(p):
+        extra = (p == 1) | (p == 2)
         halo_part(2 * p)
-        pl.when(p < PAIRS - 1)(lambda: relay_edges(p + 1))
+        pl.when(p < LOOPS - 1)(lambda: relay_edges(p + 1))
+        pl.when(extra)(lambda: relay_edges(LOOPS + p - 1))
         own_part(2 * p + 1)
         join(2 * p)
+
+        @pl.when(p == 0)
+        def _():
+            pass_gathered(0)
+            pass_gathered(1)
+
+        @pl.when(p == 1)
+        def _():
+            pass_gathered(3)
+
         halo_part(2 * p + 1)
 
-        @pl.when(p < PAIRS - 1)
+        @pl.when(p < LOOPS - 1)
         def _():
             take_edges(p + 1)
             own_part(2 * p + 2)
 
+        pl.when(extra)(lambda: take_edges(LOOPS + p - 1))
         join(2 * p + 1)
+        pl.when(p == 0)(lambda: pass_gathered(2))
+
+        @pl.when(p == 1)
+        def _():
+            pass_gathered(4)
+            pl.loop(0, GATHERED)(turn_gathered)
+
+        pl.when((p == 2) | (p == 3))(lambda: pl.loop(2 * p - 4, 2 * p - 2)(late_part))
+
+    pl.loop(0, LATE)(late_join)
 
     @pl.loop(0, PAIRS)
     def _(p):
         for h in range(2):
-
-            @pl.when(sends[h][0])
-            def _():
-                edge_copy(h, p).wait_send()
-                halo_copy(h, 2 * p).wait_send()
-                halo_copy(h, 2 * p + 1).wait_send()
-
+            pl.when(sends[h][0])(lambda h=h: edge_copy(h, p).wait_send())
             pl.when(comes[h])(lambda h=h: pass_copy(h, p, True).wait_send())
 
-    @pl.loop(0, CHUNKS)
+    @pl.loop(0, GATHERED)
+    def _(c):
+        for i in range(3):
+            gather_copy(i, c).wait_send()
+
+    @pl.loop(0, LATE)
+    def _(c):
+        for h in range(2):
+            pl.when(sends[h][0])(lambda h=h: late_copy(h, c).wait_send())
+        late_store(c).wait()
+
+    @pl.loop(0, EARLY)
     def _(j):
+        for h in range(2):
+            pl.when(sends[h][0])(lambda h=h: halo_copy(h, j).wait_send())
         for i in range(2):
             near_copy(i, j).wait_send()
+        own_copy(j).wait()
         far_copy(j).wait()
-        own_copy(j).wait()
+
+    blank_copy.wait()
 
 
 def on_device(chaos_field, mean_field, kl_fields, pattern, coupling, slot_mode):
@@ -360,15 +510,23 @@
             pltpu.VMEM((TERMS, SLOTS, SLOTS), jnp.int32),
             pltpu.VMEM((TERMS, SLOTS, SLOTS), F32),
             pltpu.VMEM((1, SLOTS), jnp.int32),
-            pltpu.VMEM((3, 2, GROUPS * PAD, DEPTH), BF16),
+            pltpu.VMEM((3, 2 * MIXED, DEPTH), BF16),
+            pltpu.VMEM((3, DEPTH, DENSE), BF16),
             pltpu.VMEM((2, CHUNKS, QUOTA, ROWS, SIDE), F32),
             pltpu.VMEM((2, CHUNKS, TERMS, ROWS, SIDE), F32),
-            pltpu.VMEM((7, TERMS, ROWS, SIDE), F32),
-            pltpu.VMEM((ROWS, GROUPS * PAD, SIDE), F32),
+            pltpu.VMEM((2, 7, TERMS, ROWS, SIDE), F32),
+            pltpu.VMEM((ROWS, MIXED, SIDE), F32),
             pltpu.VMEM((CHUNKS, GROUPS, QUOTA, ROWS, SIDE), F32),
-            pltpu.VMEM((CHUNKS, 2, QUOTA, ROWS, SIDE), F32),
+            pltpu.VMEM((EARLY, 2, QUOTA, ROWS, SIDE), F32),
+            pltpu.VMEM((GATHERED, GROUPS, QUOTA, ROWS, SIDE), F32),
+            pltpu.VMEM((GATHERED * ROWS + 1, DENSE, SIDE), BF16),
+            pltpu.VMEM((2, ROWS + 2, DEPTH, SIDE), F32),
+            pltpu.VMEM((QUOTA, LATE * ROWS, SIDE), F32),
             dma((6,)),
             dma((CHUNKS,)),
+            dma,
+            dma((3, GATHERED)),
+            dma((3, GATHERED)),
             dma((2, CHUNKS)),
             dma((2, CHUNKS)),
             dma((2, PAIRS)),
@@ -381,7 +539,7 @@
             dma((CHUNKS,)),
         ],
         compiler_params=pltpu.CompilerParams(
-            collective_id=0, has_side_effects=True, vmem_limit_bytes=40 << 20
+            collective_id=0, has_side_effects=True, vmem_limit_bytes=48 << 20
         ),
     )(*operands)
     return (own + far).reshape(QUOTA, 1, SIDE, SIDE)

time: 54.1 us -> 49.8 us (0.921)
  Pallas kernels: 52.7 us -> 48.3 us
    pallas_call x1, Pallas kernels: 52.7 us -> 48.3 us  [on_device(): pl.pallas_call(kernel, out_shape=(result, result), in_specs=[pl.BlockSpec...]
where the time goes in v1:
time: 49.8 us; the launch traced here: 49.6 us
  Pallas kernels  48.3 us (97%)
  other arithmetic  1.27 us (3%)
    pallas_call x1, Pallas kernels, on_device(): pl.pallas_call(kernel, out_shape=(result, result), in_specs=[pl.BlockSpec...  48.3 us
    reshape x1, other arithmetic, on_device(): return (own + far).reshape(QUOTA, 1, SIDE, SIDE)  1.27 us

profile of v1, /device:TPU:6, one launch (start us, length us, event | category | flops | bytes accessed | tf_op | source)
XLA Modules:
  0.0 49.6 jit_solution(10567194615537315899)
XLA Ops:
  0.0 48.3 %shard_map.64 = (f32[21,128,128]{2,1,0:T(8,128)S(1)}, f32[21,128,128]{2,1,0:T(8,128)S(1)}) custom-call(f32[21,1,128,128]{3,2,1,0:T(8,128)} %u_hbm.1, f32[1,128,128]{2,1,0:T(8,128)} %mean_hbm.1, f32[6,1,128,128]{3,2,1,0:T(8,128)} %kl_hbm.1, s32[7,84,84]{2,1,0:T(8,128)} %pattern_hbm.1, f32[7,84,84]{2,1,0:T(8,128)} %coupling_hbm.1, s32[1,84]{1,0:T(1,128)} %bitcast.5), custom_call_target="tpu_custom_call" | custom-call | tf_op jit(solution)/shard_map/pallas_call | solution.py:501
  48.3 1.3 %add_bitcast_fusion = f32[21,1,128,128]{3,2,1,0:T(8,128)} fusion(f32[21,128,128]{2,1,0:T(8,128)S(1)} %get-tuple-element.7, f32[21,128,128]{2,1,0:T(8,128)S(1)} %get-tuple-element.8), kind=kLoop, calls=%fused_computation | loop fusion | flops 344064 | bytes 4128768 | tf_op jit(solution)/shard_map/reshape | solution.py:545

commit v2 on v1

--- a/solution.py
+++ b/solution.py
@@ -161,6 +161,9 @@
     loads[2].wait()
     pl.semaphore_wait(barrier, 2 + has_up.astype(jnp.int32) + has_down.astype(jnp.int32))
 
+    def rows_of(j):
+        return pl.ds(pl.multiple_of(j * ROWS, ROWS), ROWS)
+
     def halo_copy(h, j):
         return pltpu.make_async_remote_copy(
             src_ref=u_hbm.at[:, 0, pl.ds(pl.multiple_of(j * ROWS, ROWS), ROWS)],
@@ -203,9 +206,6 @@
             device_id_type=MESH,
         )
 
-    def rows_of(j):
-        return pl.ds(pl.multiple_of(j * ROWS, ROWS), ROWS)
-
     def far_copy(j):
         return pltpu.make_async_remote_copy(
             src_ref=partial.at[j, across],
@@ -238,7 +238,7 @@
     def late_copy(h, c):
         return pltpu.make_async_remote_copy(
             src_ref=partial.at[EARLY + c, h],
-            dst_ref=halo.at[h, EARLY + c],
+            dst_ref=halo.at[1, EARLY + c] if h == 1 else far_out.at[:, rows_of(EARLY + c)],
             send_sem=halo_send.at[h, EARLY + c],
             recv_sem=halo_recv.at[h, EARLY + c],
             device_id=sends[h][1],
@@ -260,9 +260,13 @@
         gather_copy(0, c).start()
         gather_copy(1, c).start()
 
-    blank[...] = jnp.zeros_like(blank)
     blank_copy = pltpu.make_async_copy(blank, far_out.at[:, pl.ds(EARLY * ROWS, LATE * ROWS)], blank_sem)
-    blank_copy.start()
+
+    @pl.when(jnp.logical_not(has_down))
+    def _():
+        blank[...] = jnp.zeros_like(blank)
+        blank_copy.start()
+
     dense[GATHERED * ROWS] = jnp.zeros((DENSE, SIDE), BF16)
 
     loads[3].wait()
@@ -413,9 +417,8 @@
 
     def late_join(c):
         j = EARLY + c
-        for h in range(2):
-            pl.when(comes[h])(lambda h=h: late_copy(h, c).wait_recv())
-        partial[j, 2] = partial[j, 2] + halo[0, j] + halo[1, j]
+        pl.when(has_up)(lambda: late_copy(1, c).wait_recv())
+        partial[j, 2] = partial[j, 2] + halo[1, j]
         late_store(c).start()
 
     def late_store(c):
@@ -429,10 +432,12 @@
     @pl.loop(0, LOOPS)
     def _(p):
         extra = (p == 1) | (p == 2)
+        late = (p == 2) | (p == 3)
         halo_part(2 * p)
         pl.when(p < LOOPS - 1)(lambda: relay_edges(p + 1))
         pl.when(extra)(lambda: relay_edges(LOOPS + p - 1))
         own_part(2 * p + 1)
+        pl.when(late)(lambda: late_part(2 * p - 4))
         join(2 * p)
 
         @pl.when(p == 0)
@@ -452,6 +457,7 @@
             own_part(2 * p + 2)
 
         pl.when(extra)(lambda: take_edges(LOOPS + p - 1))
+        pl.when(late)(lambda: late_part(2 * p - 3))
         join(2 * p + 1)
         pl.when(p == 0)(lambda: pass_gathered(2))
 
@@ -460,9 +466,6 @@
             pass_gathered(4)
             pl.loop(0, GATHERED)(turn_gathered)
 
-        pl.when((p == 2) | (p == 3))(lambda: pl.loop(2 * p - 4, 2 * p - 2)(late_part))
-
-    pl.loop(0, LATE)(late_join)
 
     @pl.loop(0, PAIRS)
     def _(p):
@@ -475,22 +478,28 @@
         for i in range(3):
             gather_copy(i, c).wait_send()
 
-    @pl.loop(0, LATE)
-    def _(c):
-        for h in range(2):
-            pl.when(sends[h][0])(lambda h=h: late_copy(h, c).wait_send())
-        late_store(c).wait()
-
     @pl.loop(0, EARLY)
     def _(j):
         for h in range(2):
             pl.when(sends[h][0])(lambda h=h: halo_copy(h, j).wait_send())
         for i in range(2):
             near_copy(i, j).wait_send()
+
+    pl.when(jnp.logical_not(has_down))(blank_copy.wait)
+
+    pl.loop(0, LATE)(late_join)
+
+    @pl.loop(0, EARLY)
+    def _(j):
         own_copy(j).wait()
         far_copy(j).wait()
 
-    blank_copy.wait()
+    @pl.loop(0, LATE)
+    def _(c):
+        for h in range(2):
+            pl.when(sends[h][0])(lambda h=h: late_copy(h, c).wait_send())
+        late_store(c).wait()
+        pl.when(has_down)(lambda: late_copy(0, c).wait_recv())
 
 
 def on_device(chaos_field, mean_field, kl_fields, pattern, coupling, slot_mode):

time: 49.8 us -> 48.6 us (0.976)
  Pallas kernels: 48.3 us -> 47.2 us
    pallas_call x1, Pallas kernels: 48.3 us -> 47.2 us  [on_device(): pl.pallas_call(kernel, out_shape=(result, result), in_specs=[pl.BlockSpec...]
where the time goes in v2:
time: 48.6 us; the launch traced here: 48.5 us
  Pallas kernels  47.2 us (97%)
  other arithmetic  1.27 us (3%)
    pallas_call x1, Pallas kernels, on_device(): pl.pallas_call(kernel, out_shape=(result, result), in_specs=[pl.BlockSpec...  47.2 us
    reshape x1, other arithmetic, on_device(): return (own + far).reshape(QUOTA, 1, SIDE, SIDE)  1.27 us

profile of v2, /device:TPU:6, one launch (start us, length us, event | category | flops | bytes accessed | tf_op | source)
XLA Modules:
  0.0 48.5 jit_solution(15418350662126557482)
XLA Ops:
  0.0 47.2 %shard_map.64 = (f32[21,128,128]{2,1,0:T(8,128)S(1)}, f32[21,128,128]{2,1,0:T(8,128)S(1)}) custom-call(f32[21,1,128,128]{3,2,1,0:T(8,128)} %u_hbm.1, f32[1,128,128]{2,1,0:T(8,128)} %mean_hbm.1, f32[6,1,128,128]{3,2,1,0:T(8,128)} %kl_hbm.1, s32[7,84,84]{2,1,0:T(8,128)} %pattern_hbm.1, f32[7,84,84]{2,1,0:T(8,128)} %coupling_hbm.1, s32[1,84]{1,0:T(1,128)} %bitcast.5), custom_call_target="tpu_custom_call" | custom-call | tf_op jit(solution)/shard_map/pallas_call | solution.py:510
  47.2 1.3 %add_bitcast_fusion = f32[21,1,128,128]{3,2,1,0:T(8,128)} fusion(f32[21,128,128]{2,1,0:T(8,128)S(1)} %get-tuple-element.7, f32[21,128,128]{2,1,0:T(8,128)S(1)} %get-tuple-element.8), kind=kLoop, calls=%fused_computation | loop fusion | flops 344064 | bytes 4128768 | tf_op jit(solution)/shard_map/reshape | solution.py:554

commit v3 on v2

--- a/solution.py
+++ b/solution.py
@@ -101,7 +101,7 @@
     field, turned, coef, pattern, coupling, slots, mixing, turned_mixing, halo, edge, weight, centre, partial, near,
     gathered, dense, mixed_rows, blank,
     load_sem, store_sem, blank_sem,
-    gather_send, gather_recv,
+    gather_send, gather_recv, share_send, share_recv,
     halo_send, halo_recv, edge_send, edge_recv, pass_send, pass_recv, near_send, near_recv, far_send, far_recv,
 ):
     place = lax.axis_index("space")
@@ -118,6 +118,9 @@
     has_down = place > 0
     up = (place + 1, mode_up)
     down = (place - 1, mode_down)
+    level = mode // 2
+    shared_in = along == 0
+    shared_out = along == RING - 1
     sends = ((has_up, up), (has_down, down))
     comes = (has_down, has_up)
 
@@ -137,8 +140,11 @@
     def greet(device):
         pl.semaphore_signal(barrier, inc=1, device_id=device, device_id_type=MESH)
 
-    for there, device in sends:
-        pl.when(there)(lambda device=device: greet(device))
+    first_place, last_place = along == 0, along == RING - 1
+    invites = has_down & first_place
+    accepts = has_up & last_place
+    pl.when(has_up & jnp.logical_not(last_place))(lambda: greet(up))
+    pl.when(has_down & jnp.logical_not(first_place))(lambda: greet(down))
     greet((place, sibling))
     greet((place, across))
 
@@ -159,7 +165,10 @@
 
     loads[1].wait()
     loads[2].wait()
-    pl.semaphore_wait(barrier, 2 + has_up.astype(jnp.int32) + has_down.astype(jnp.int32))
+    count = 2 + has_up.astype(jnp.int32) + has_down.astype(jnp.int32) - invites.astype(jnp.int32)
+    pl.semaphore_wait(barrier, count)
+    pl.when(invites)(lambda: greet(down))
+    pl.when(accepts)(lambda: greet(up))
 
     def rows_of(j):
         return pl.ds(pl.multiple_of(j * ROWS, ROWS), ROWS)
@@ -196,6 +205,17 @@
             device_id_type=MESH,
         )
 
+    def share_copy(p):
+        j = 2 * p + core
+        return pltpu.make_async_remote_copy(
+            src_ref=edge.at[0, j],
+            dst_ref=edge.at[0, j],
+            send_sem=share_send.at[p],
+            recv_sem=share_recv.at[p],
+            device_id=(place, across),
+            device_id_type=MESH,
+        )
+
     def near_copy(i, j):
         return pltpu.make_async_remote_copy(
             src_ref=partial.at[j, (sibling, diagonal)[i]],
@@ -219,9 +239,9 @@
     def own_copy(j):
         return pltpu.make_async_copy(partial.at[j, mode], own_out.at[:, rows_of(j)], store_sem.at[j])
 
-    def send_edges(p):
-        for h in range(2):
-            pl.when(sends[h][0])(lambda h=h: edge_copy(h, p).start())
+    def send_edges(p, now):
+        pl.when(now[0] & jnp.logical_not(shared_out))(lambda: edge_copy(0, p).start())
+        pl.when(now[1])(lambda: edge_copy(1, p).start())
 
     def gather_copy(i, c):
         rows = pl.ds(pl.multiple_of((EARLY - 1 + c) * ROWS, ROWS), ROWS)
@@ -245,15 +265,27 @@
             device_id_type=MESH,
         )
 
-    send_edges(0)
-
-    @pl.loop(0, LOOPS)
-    def _(p):
-        pl.when(p < LOOPS - 1)(lambda: send_edges(p + 1))
-        pl.when((p == 1) | (p == 2))(lambda: send_edges(LOOPS + p - 1))
-        for j in (2 * p, 2 * p + 1):
-            for h in range(2):
-                pl.when(sends[h][0])(lambda h=h, j=j: halo_copy(h, j).start())
+    goes = has_up & shared_out
+    comes_shared = has_down & shared_in
+
+    @pl.when(goes)
+    def _():
+        @pl.loop(0, PAIRS // 2)
+        def _(q):
+            edge_copy(0, 2 * q + mode_up // 2).start()
+
+    def send_all(now):
+        send_edges(0, now)
+
+        @pl.loop(0, LOOPS)
+        def _(p):
+            pl.when(p < LOOPS - 1)(lambda: send_edges(p + 1, now))
+            pl.when((p == 1) | (p == 2))(lambda: send_edges(LOOPS + p - 1, now))
+            for j in (2 * p, 2 * p + 1):
+                for h in range(2):
+                    pl.when(now[h])(lambda h=h, j=j: halo_copy(h, j).start())
+
+    send_all((has_up, has_down & jnp.logical_not(first_place)))
 
     @pl.loop(0, GATHERED)
     def _(c):
@@ -279,12 +311,21 @@
     def _(j):
         turned[pl.ds(j * ROWS + 1, ROWS)] = slots_inside(field[:, rows_of(j)])
 
+    @pl.when(invites)
+    def _():
+        pl.semaphore_wait(barrier, 1)
+        send_all((place < 0, has_down))
+
     def relay_edges(p):
         for h in range(2):
 
             @pl.when(comes[h])
             def _():
-                edge_copy(h, p).wait_recv()
+                if h == 0:
+                    pl.when(jnp.logical_not(shared_in))(lambda: edge_copy(0, p).wait_recv())
+                    pl.when(shared_in & (p % 2 != level))(lambda: share_copy(p).wait_recv())
+                else:
+                    edge_copy(1, p).wait_recv()
                 pass_copy(h, p, True).start()
 
     def take_edges(p):
@@ -425,6 +466,13 @@
         j = EARLY + c
         return pltpu.make_async_copy(partial.at[j, 2], own_out.at[:, rows_of(j)], store_sem.at[j])
 
+    @pl.when(comes_shared)
+    def _():
+        @pl.loop(0, PAIRS // 2)
+        def _(q):
+            edge_copy(0, 2 * q + level).wait_recv()
+            share_copy(2 * q + level).start()
+
     relay_edges(0)
     take_edges(0)
     own_part(0)
@@ -434,11 +482,11 @@
         extra = (p == 1) | (p == 2)
         late = (p == 2) | (p == 3)
         halo_part(2 * p)
+        pl.when(p > 0)(lambda: join(2 * p - 1))
         pl.when(p < LOOPS - 1)(lambda: relay_edges(p + 1))
         pl.when(extra)(lambda: relay_edges(LOOPS + p - 1))
         own_part(2 * p + 1)
         pl.when(late)(lambda: late_part(2 * p - 4))
-        join(2 * p)
 
         @pl.when(p == 0)
         def _():
@@ -450,6 +498,7 @@
             pass_gathered(3)
 
         halo_part(2 * p + 1)
+        join(2 * p)
 
         @pl.when(p < LOOPS - 1)
         def _():
@@ -458,7 +507,6 @@
 
         pl.when(extra)(lambda: take_edges(LOOPS + p - 1))
         pl.when(late)(lambda: late_part(2 * p - 3))
-        join(2 * p + 1)
         pl.when(p == 0)(lambda: pass_gathered(2))
 
         @pl.when(p == 1)
@@ -467,11 +515,16 @@
             pl.loop(0, GATHERED)(turn_gathered)
 
 
+    join(EARLY - 1)
+
     @pl.loop(0, PAIRS)
     def _(p):
         for h in range(2):
-            pl.when(sends[h][0])(lambda h=h: edge_copy(h, p).wait_send())
             pl.when(comes[h])(lambda h=h: pass_copy(h, p, True).wait_send())
+
+        pl.when(has_up & (jnp.logical_not(shared_out) | (p % 2 == mode_up // 2)))(lambda: edge_copy(0, p).wait_send())
+        pl.when(has_down)(lambda: edge_copy(1, p).wait_send())
+        pl.when(comes_shared & (p % 2 == level))(lambda: share_copy(p).wait_send())
 
     @pl.loop(0, GATHERED)
     def _(c):
@@ -536,6 +589,8 @@
             dma,
             dma((3, GATHERED)),
             dma((3, GATHERED)),
+            dma((PAIRS,)),
+            dma((PAIRS,)),
             dma((2, CHUNKS)),
             dma((2, CHUNKS)),
             dma((2, PAIRS)),

time: 48.6 us -> 48.2 us (level)
  no operation moved by 1% of the time
where the time goes in v3:
time: 48.2 us; the launch traced here: 48.1 us
  Pallas kernels  46.8 us (97%)
  other arithmetic  1.27 us (3%)
    pallas_call x1, Pallas kernels, on_device(): pl.pallas_call(kernel, out_shape=(result, result), in_specs=[pl.BlockSpec...  46.8 us
    reshape x1, other arithmetic, on_device(): return (own + far).reshape(QUOTA, 1, SIDE, SIDE)  1.27 us

profile of v3, /device:TPU:6, one launch (start us, length us, event | category | flops | bytes accessed | tf_op | source)
XLA Modules:
  0.0 48.1 jit_solution(15405213250839483581)
XLA Ops:
  0.0 46.8 %shard_map.64 = (f32[21,128,128]{2,1,0:T(8,128)S(1)}, f32[21,128,128]{2,1,0:T(8,128)S(1)}) custom-call(f32[21,1,128,128]{3,2,1,0:T(8,128)} %u_hbm.1, f32[1,128,128]{2,1,0:T(8,128)} %mean_hbm.1, f32[6,1,128,128]{3,2,1,0:T(8,128)} %kl_hbm.1, s32[7,84,84]{2,1,0:T(8,128)} %pattern_hbm.1, f32[7,84,84]{2,1,0:T(8,128)} %coupling_hbm.1, s32[1,84]{1,0:T(1,128)} %bitcast.5), custom_call_target="tpu_custom_call" | custom-call | tf_op jit(solution)/shard_map/pallas_call | solution.py:563
  46.8 1.3 %add_bitcast_fusion = f32[21,1,128,128]{3,2,1,0:T(8,128)} fusion(f32[21,128,128]{2,1,0:T(8,128)S(1)} %get-tuple-element.7, f32[21,128,128]{2,1,0:T(8,128)S(1)} %get-tuple-element.8), kind=kLoop, calls=%fused_computation | loop fusion | flops 344064 | bytes 4128768 | tf_op jit(solution)/shard_map/reshape | solution.py:609

commit v4 on v3

--- a/solution.py
+++ b/solution.py
@@ -163,8 +163,6 @@
                 halo[h, j] = jnp.zeros((QUOTA, ROWS, SIDE), F32)
                 edge[h, j] = zero_rows
 
-    loads[1].wait()
-    loads[2].wait()
     count = 2 + has_up.astype(jnp.int32) + has_down.astype(jnp.int32) - invites.astype(jnp.int32)
     pl.semaphore_wait(barrier, count)
     pl.when(invites)(lambda: greet(down))
@@ -265,6 +263,11 @@
             device_id_type=MESH,
         )
 
+    first_now = (has_up, has_down & jnp.logical_not(first_place))
+    for h in range(2):
+        pl.when(first_now[h])(lambda h=h: halo_copy(h, 0).start())
+    loads[1].wait()
+    loads[2].wait()
     goes = has_up & shared_out
     comes_shared = has_down & shared_in
 
@@ -274,7 +277,7 @@
         def _(q):
             edge_copy(0, 2 * q + mode_up // 2).start()
 
-    def send_all(now):
+    def send_all(now, start):
         send_edges(0, now)
 
         @pl.loop(0, LOOPS)
@@ -283,9 +286,9 @@
             pl.when((p == 1) | (p == 2))(lambda: send_edges(LOOPS + p - 1, now))
             for j in (2 * p, 2 * p + 1):
                 for h in range(2):
-                    pl.when(now[h])(lambda h=h, j=j: halo_copy(h, j).start())
-
-    send_all((has_up, has_down & jnp.logical_not(first_place)))
+                    pl.when(now[h] & (j >= start))(lambda h=h, j=j: halo_copy(h, j).start())
+
+    send_all(first_now, 1)
 
     @pl.loop(0, GATHERED)
     def _(c):
@@ -314,7 +317,7 @@
     @pl.when(invites)
     def _():
         pl.semaphore_wait(barrier, 1)
-        send_all((place < 0, has_down))
+        send_all((place < 0, has_down), 0)
 
     def relay_edges(p):
         for h in range(2):
@@ -466,16 +469,21 @@
         j = EARLY + c
         return pltpu.make_async_copy(partial.at[j, 2], own_out.at[:, rows_of(j)], store_sem.at[j])
 
+    def share(q):
+        edge_copy(0, 2 * q + level).wait_recv()
+        share_copy(2 * q + level).start()
+
     @pl.when(comes_shared)
     def _():
-        @pl.loop(0, PAIRS // 2)
-        def _(q):
-            edge_copy(0, 2 * q + level).wait_recv()
-            share_copy(2 * q + level).start()
+        share(0)
 
     relay_edges(0)
     take_edges(0)
     own_part(0)
+
+    @pl.when(comes_shared)
+    def _():
+        pl.loop(1, PAIRS // 2)(share)
 
     @pl.loop(0, LOOPS)
     def _(p):

time: 48.2 us -> 49.8 us (1.033)
  Pallas kernels: 46.8 us -> 48.4 us
    pallas_call x1, Pallas kernels: 46.8 us -> 48.4 us  [on_device(): pl.pallas_call(kernel, out_shape=(result, result), in_specs=[pl.BlockSpec...]
where the time goes in v4:
time: 49.8 us; the launch traced here: 49.7 us
  Pallas kernels  48.4 us (97%)
  other arithmetic  1.27 us (3%)
    pallas_call x1, Pallas kernels, on_device(): pl.pallas_call(kernel, out_shape=(result, result), in_specs=[pl.BlockSpec...  48.4 us
    reshape x1, other arithmetic, on_device(): return (own + far).reshape(QUOTA, 1, SIDE, SIDE)  1.27 us

profile of v4, /device:TPU:6, one launch (start us, length us, event | category | flops | bytes accessed | tf_op | source)
XLA Modules:
  0.0 49.7 jit_solution(11496928928439494712)
XLA Ops:
  0.0 48.4 %shard_map.64 = (f32[21,128,128]{2,1,0:T(8,128)S(1)}, f32[21,128,128]{2,1,0:T(8,128)S(1)}) custom-call(f32[21,1,128,128]{3,2,1,0:T(8,128)} %u_hbm.1, f32[1,128,128]{2,1,0:T(8,128)} %mean_hbm.1, f32[6,1,128,128]{3,2,1,0:T(8,128)} %kl_hbm.1, s32[7,84,84]{2,1,0:T(8,128)} %pattern_hbm.1, f32[7,84,84]{2,1,0:T(8,128)} %coupling_hbm.1, s32[1,84]{1,0:T(1,128)} %bitcast.5), custom_call_target="tpu_custom_call" | custom-call | tf_op jit(solution)/shard_map/pallas_call | solution.py:571
  48.4 1.3 %add_bitcast_fusion = f32[21,1,128,128]{3,2,1,0:T(8,128)} fusion(f32[21,128,128]{2,1,0:T(8,128)S(1)} %get-tuple-element.7, f32[21,128,128]{2,1,0:T(8,128)S(1)} %get-tuple-element.8), kind=kLoop, calls=%fused_computation | loop fusion | flops 344064 | bytes 4128768 | tf_op jit(solution)/shard_map/reshape | solution.py:617
